TPU v7x, 128 devices: a whole 4x4x4 slice. The times are simulated.
128 devices in a mesh: grp: 4 (over z), ep: 32 (over x, y, core).
Axes of the slice: x: 4, y: 4, z: 4, core: 2. Of those that a mesh axis runs over, the one named last changes fastest.
Arguments:
- attention: bfloat16 [16384, 1024], P(('grp', 'ep')), may hold values from -6 to 6
- residual: bfloat16 [16384, 1024], P(('grp', 'ep')), may hold values from -6 to 6
- out_proj: bfloat16 [1024, 1024], P(None, 'grp'), may hold values from -0.1875 to 0.1875
- pre_gain: float32 [1024], replicated, may hold values from 0.25 to 1.75
- post_gain: float32 [1024], replicated, may hold values from 0.25 to 1.75
- slot_gate_up: bfloat16 [32, 1024, 1024], P('ep'), may hold values from -0.1875 to 0.1875
- slot_down: bfloat16 [32, 512, 1024], P('ep'), may hold values from -0.25 to 0.25
- expert_ids: int32 [16384, 8], P(('grp', 'ep')), may hold values from 0 to 31, all different within a row
- copy_choice: int32 [16384, 8], P(('grp', 'ep')), may hold values from 0 to 3
- placement: int32 [32], replicated, may hold values from 0 to 31, each once
- request_age: int32 [16384], P(('grp', 'ep')), may hold values from 0 to 1048575
- decode_flag: int32 [16384], P(('grp', 'ep')), may hold values 0 or 1
- capacity: int32 [4, 32], replicated, may hold values from 4 to 8, as said below
- route_weight: float32 [16384, 8], P(('grp', 'ep')), may hold values from 0.05 to 1
Outputs:
- layer_out: bfloat16 [16384, 1024], P(('grp', 'ep'))
Inputs may be any that keep to these rules, and one draw needn't show every extreme that they name: At least one block has capacity 8. `expert_ids`: each row names 8 different experts. `placement`: each slot holds a different expert.
All inputs are finite; a program needn't handle non-finite values. No bound on the sum of `decode_flag` on one device may be relied on, other than what follows from the above.
Results may differ from a plain program's by a relative error of at most 0.01.
Values may be sent and summed in bfloat16 or wider, within the bound.
A program may use at most 64 MiB of HBM per device.

v0:
```python
import jax
import jax.numpy as jnp
from jax import lax
from jax.sharding import PartitionSpec as P


def rms_scale(values, gain):
    meansq = jnp.mean(values * values, axis=-1, keepdims=True)
    return values * lax.rsqrt(meansq + 1e-06) * gain


def on_device(
    attention,
    residual,
    out_proj,
    pre_gain,
    post_gain,
    slot_gate_up,
    slot_down,
    expert_ids,
    copy_choice,
    placement,
    request_age,
    decode_flag,
    capacity,
    route_weight,
):
    groups = lax.axis_size("grp")
    owners = lax.axis_size("ep")
    devices_all = groups * owners
    rows_here = attention.shape[0]
    features = attention.shape[1]
    picks_row = expert_ids.shape[1]
    cap_size = max(2, rows_here * picks_row // devices_all)
    columns = jnp.dot(
        lax.all_gather(attention, "grp", axis=0, tiled=True),
        out_proj,
        preferred_element_type=jnp.float32,
    )
    attn_proj = lax.all_to_all(columns, "grp", split_axis=0, concat_axis=1, tiled=True)
    hidden_state = (residual.astype(jnp.float32) + attn_proj).astype(jnp.bfloat16)
    normed = rms_scale(hidden_state.astype(jnp.float32), pre_gain).astype(jnp.bfloat16)
    experts_all = placement.shape[0]
    slot_table = jnp.arange(owners, dtype=jnp.int32)
    matches = (placement[None, :] == jnp.arange(experts_all, dtype=jnp.int32)[:, None]).astype(
        jnp.int32
    )
    slot_of = jnp.sum(slot_table[None, :] * matches, axis=1)
    expert_hits = (
        expert_ids[:, :, None] == jnp.arange(experts_all, dtype=jnp.int32)[None, None, :]
    ).astype(jnp.int32)
    target = copy_choice * owners + jnp.sum(expert_hits * slot_of[None, None, :], axis=2)
    priority = decode_flag * 1048576 + request_age
    order = jnp.arange(rows_here, dtype=jnp.int32)
    ahead_mask = (priority[None, :] > priority[:, None]) | (
        priority[None, :] == priority[:, None]
    ) & (order[None, :] < order[:, None])
    target_hits = jnp.sum(
        (target[:, :, None] == jnp.arange(devices_all, dtype=jnp.int32)[None, None, :]).astype(
            jnp.bfloat16
        ),
        axis=1,
    )
    counts = jnp.dot(
        ahead_mask.astype(jnp.bfloat16), target_hits, preferred_element_type=jnp.float32
    )
    position = jnp.take_along_axis(counts, target, axis=1).astype(jnp.int32)
    granted = jnp.take(capacity.reshape(-1), target)
    accepted = position < granted
    total_slots = devices_all * cap_size
    index = jnp.where(accepted, target * cap_size + position, total_slots)
    spread_rows = jnp.broadcast_to(normed[:, None, :], (rows_here, picks_row, features)).reshape(
        rows_here * picks_row, features
    )
    buffer = (
        jnp.zeros((total_slots, features), jnp.bfloat16)
        .at[index.reshape(-1)]
        .set(spread_rows, mode="drop")
    )
    gate_up_local = slot_gate_up[0]
    down_local = slot_down[0]
    hidden_units = down_local.shape[0]
    arrived = lax.all_to_all(
        buffer.reshape(devices_all, cap_size, features),
        ("grp", "ep"),
        split_axis=0,
        concat_axis=0,
        tiled=True,
    )
    flattened = arrived.reshape(-1, features)
    gate_up = jnp.dot(flattened, gate_up_local, preferred_element_type=jnp.float32)
    expert_hidden = (jax.nn.silu(gate_up[:, :hidden_units]) * gate_up[:, hidden_units:]).astype(
        jnp.bfloat16
    )
    produced = jnp.dot(expert_hidden, down_local, preferred_element_type=jnp.float32).astype(
        jnp.bfloat16
    )
    returned = lax.all_to_all(
        produced.reshape(arrived.shape), ("grp", "ep"), split_axis=0, concat_axis=0, tiled=True
    )
    flat_back = returned.reshape(total_slots, features)
    expert_out = flat_back[jnp.minimum(index, total_slots - 1)]
    weights_kept = jnp.where(accepted, route_weight, jnp.float32(0.0))
    mixture = jnp.einsum("rk,rkd->rd", weights_kept, expert_out, preferred_element_type=jnp.float32)
    return rms_scale(hidden_state.astype(jnp.float32) + mixture, post_gain).astype(jnp.bfloat16)


def solution(mesh):
    placed = (
        P(("grp", "ep"), None),
        P(("grp", "ep"), None),
        P(None, "grp"),
        P(),
        P(),
        P("ep", None, None),
        P("ep", None, None),
        P(("grp", "ep"), None),
        P(("grp", "ep"), None),
        P(),
        P(("grp", "ep")),
        P(("grp", "ep")),
        P(),
        P(("grp", "ep"), None),
    )
    return jax.shard_map(
        on_device, mesh=mesh, in_specs=placed, out_specs=P(("grp", "ep"), None), check_vma=False
    )
```

profile of v0, /device:TPU:1, one launch (start us, length us, event | category | flops | bytes accessed | tf_op | source)
XLA Modules:
  0.0 155.6 jit_solution(14246727109927637221)
XLA Ops:
  6.5 0.0 copy-start
  6.5 0.0 all-gather.2.cloned.1.call-start
  6.5 0.7 all-gather.2.cloned.1.call-update
  7.3 0.8 select_reduce_fusion.1
  8.0 0.8 select_reduce_fusion
  8.8 0.7 bitcast_or_fusion
  9.5 0.1 copy.24
  9.6 0.1 copy.25
  9.7 0.1 reshape.110
  9.8 0.2 fusion.17
  10.1 0.7 multiply_add_fusion.1
  10.7 0.2 fusion.20
  10.9 0.0 copy-start.6
  10.9 6.8 %gather_fusion.2 = f32[1024]{0:T(1024)S(1)} fusion(f32[128,128]{1,0:T(8,128)S(1)} %fusion.20, s32[1024]{0:T(1024)S(1)} %reshape.110), kind=kCustom, calls=%fused_computation.2 | custom fusion | bytes 16384 | tf_op jit(solution)/shard_map/jit(take_along_axis)/gather | solution.py:67
  17.8 0.1 reshape.113
  17.9 0.1 copy.27
  18.0 0.1 reshape.96
  18.1 0.0 copy-done.6
  18.1 0.1 reshape.87
  18.2 0.0 copy-start.1
  18.2 6.6 %gather_fusion = s32[1024]{0:T(1024)S(1)} fusion(s32[128]{0:T(128)S(1)} %reshape.87, s32[1024]{0:T(1024)S(1)} %broadcast_clamp_fusion.1), kind=kCustom, calls=%fused_computation | custom fusion | bytes 12288 | tf_op jit(solution)/shard_map/jit(_take)/gather | solution.py:68
  24.8 0.1 reshape.95
  24.9 0.0 copy-start.2
  24.9 10.7 %all-gather.2.cloned.1.call-done = bf16[512,1024]{1,0:T(8,128)(2,1)} async-done(((bf16[128,1024]{1,0:T(8,128)(2,1)}), bf16[512,1024]{1,0:T(8,128)(2,1)}) %all-gather.2.cloned.1.call-update) | async-done | bytes 1048592 | tf_op jit(solution)/shard_map/all_gather | solution.py:36
  35.6 0.0 copy-done.1
  35.6 2.5 %fusion.27 = f32[512,256]{1,0:T(8,128)} fusion(bf16[512,1024]{1,0:T(8,128)(2,1)} %all-gather.2.cloned.1.call-done, bf16[1024,256]{1,0:T(8,128)(2,1)S(1)} %copy-done.1), kind=kOutput, calls=%fused_computation.57 | convolution fusion | flops 268435456 | bytes 2097152 | tf_op jit(solution)/shard_map/dot_general | solution.py:35
  38.1 0.0 copy-start.3
  38.1 3.6 %all-to-all-start = ((f32[4,128,256]{2,1,0:T(8,128)}), f32[4,128,256]{2,1,0:T(8,128)S(1)}, u32[]{:S(2)}, u32[]{:S(2)}) async-start(f32[4,128,256]{2,1,0:T(8,128)} %bitcast), calls=%async_computation | async-start | bytes 1048576 | tf_op jit(solution)/shard_map/all_to_all | solution.py:40
  41.7 0.1 copy.29
  41.8 0.1 reshape.88
  41.9 7.3 %all-to-all-done = f32[4,128,256]{2,1,0:T(8,128)S(1)} async-done(((f32[4,128,256]{2,1,0:T(8,128)}), f32[4,128,256]{2,1,0:T(8,128)S(1)}, u32[]{:S(2)}, u32[]{:S(2)}) %all-to-all-start) | async-done | bytes 524320 | tf_op jit(solution)/shard_map/all_to_all | solution.py:40
  49.2 0.0 copy-done.2
  49.2 0.2 fusion.13
  49.4 0.0 copy-done.3
  49.4 0.1 fusion.15
  49.6 6.8 %scatter_custom_fusion = bf16[1024,1024]{1,0:T(8,128)(2,1)} fusion(s32[1024]{0:T(1024)S(1)} %bitcast.43, bf16[128,1024]{1,0:T(8,128)(2,1)S(1)} %fusion.15, bf16[]{:T(256)} %constant.29.clone.1), kind=kCustom, calls=%fused_computation.11 | custom fusion | bytes 2359298 | tf_op jit(solution)/shard_map/scatter | solution.py:78
  56.4 40.3 %all_to_all.29 = bf16[128,8,1024]{2,1,0:T(8,128)(2,1)S(1)} all-to-all(bf16[128,8,1024]{2,1,0:T(8,128)(2,1)} %bitcast.40), channel_id=1, replica_groups=mesh['grp'=4,'ep'=32] {'grp','ep'}, dimensions={0} | all-to-all | bytes 4194304 | tf_op jit(solution)/shard_map/all_to_all | solution.py:83
  96.7 0.0 copy-done
  96.7 0.0 copy-start.7
  96.7 2.4 %fusion.3 = f32[1024,1024]{1,0:T(8,128)S(1)} fusion(bf16[1,1024,1024]{2,1,0:T(8,128)(2,1)S(1)} %copy-done, bf16[128,8,1024]{2,1,0:T(8,128)(2,1)S(1)} %all_to_all.29), kind=kOutput, calls=%fused_computation.8 | convolution fusion | flops 2147483648 | bytes 8388608 | tf_op jit(solution)/shard_map/dot_general | solution.py:91
  99.1 0.0 copy-done.7
  99.1 2.6 %convert_bitcast_fusion = bf16[128,8,1024]{2,1,0:T(8,128)(2,1)} fusion(f32[1024,1024]{1,0:T(8,128)S(1)} %fusion.3, bf16[1,512,1024]{2,1,0:T(8,128)(2,1)S(1)} %copy-done.7), kind=kOutput, calls=%fused_computation.13 | convolution fusion | flops 1077936128 | bytes 7340032 | tf_op jit(solution)/shard_map/dot_general | solution.py:95
  101.7 0.0 copy-start.5
  101.7 5.5 %all-to-all-start.2 = ((bf16[128,8,1024]{2,1,0:T(8,128)(2,1)}), bf16[128,8,1024]{2,1,0:T(8,128)(2,1)}, u32[]{:S(2)}, u32[]{:S(2)}) async-start(bf16[128,8,1024]{2,1,0:T(8,128)(2,1)} %convert_bitcast_fusion), calls=%async_computation.2 | async-start | bytes 4194304 | tf_op jit(solution)/shard_map/all_to_all | solution.py:98
  107.2 0.1 copy.30
  107.3 0.1 reshape.104
  107.4 0.0 copy-done.5
  107.5 0.1 copy.31
  107.6 29.9 %all-to-all-done.2 = bf16[128,8,1024]{2,1,0:T(8,128)(2,1)} async-done(((bf16[128,8,1024]{2,1,0:T(8,128)(2,1)}), bf16[128,8,1024]{2,1,0:T(8,128)(2,1)}, u32[]{:S(2)}, u32[]{:S(2)}) %all-to-all-start.2) | async-done | bytes 2097184 | tf_op jit(solution)/shard_map/all_to_all | solution.py:98
  137.5 7.9 %gather_fusion.1 = bf16[1024,1024]{1,0:T(8,128)(2,1)} fusion(bf16[1024,1024]{1,0:T(8,128)(2,1)} %bitcast.11, s32[1024]{0:T(1024)S(1)} %broadcast_clamp_fusion), kind=kCustom, calls=%fused_computation.1 | custom fusion | bytes 4198400 | tf_op jit(solution)/shard_map/gather | solution.py:102
  145.5 0.0 copy-start.4
  145.5 2.3 %fusion.1 = f32[128,1,1024]{2,1,0:T(1,128)S(1)} fusion(bf16[128,8,1]{1,2,0:T(2,128)(2,1)S(1)} %copy.31, bf16[1024,1024]{1,0:T(8,128)(2,1)} %gather_fusion.1), kind=kOutput, calls=%fused_computation.6 | convolution fusion | flops 2097152 | bytes 2623488 | tf_op jit(solution)/shard_map/rk,rkd->rd/dot_general | solution.py:104
  147.8 0.2 multiply_reduce_fusion
  147.9 0.0 copy-done.4
  147.9 0.8 multiply_convert_fusion
  (11 shorter events, 0.2 us)
Async XLA Ops:
  6.5 90.2 %copy-start = (bf16[1,1024,1024]{2,1,0:T(8,128)(2,1)S(1)}, bf16[1,1024,1024]{2,1,0:T(8,128)(2,1)}, u32[]{:S(2)}) copy-start(bf16[1,1024,1024]{2,1,0:T(8,128)(2,1)} %param.19) | copy-start | bytes 6291460
  6.5 29.1 %all-gather.2.cloned.1.call-start = ((), (), s32[]{:S(2)}) async-start(), calls=%async_computation.3 | async-start | bytes 1310720 | tf_op jit(solution)/shard_map/all_gather | solution.py:36
  10.9 7.2 %copy-start.6 = (s32[4,32]{1,0:T(4,128)S(1)}, s32[4,32]{1,0:T(4,128)}, u32[]{:S(2)}) copy-start(s32[4,32]{1,0:T(4,128)} %param.26) | copy-start | bytes 1540
  18.2 17.4 %copy-start.1 = (bf16[1024,256]{1,0:T(8,128)(2,1)S(1)}, bf16[1024,256]{1,0:T(8,128)(2,1)}, u32[]{:S(2)}) copy-start(bf16[1024,256]{1,0:T(8,128)(2,1)} %param.16) | copy-start | bytes 1572868
  24.9 24.3 %copy-start.2 = (bf16[128,1024]{1,0:T(8,128)(2,1)S(1)}, bf16[128,1024]{1,0:T(8,128)(2,1)}, u32[]{:S(2)}) copy-start(bf16[128,1024]{1,0:T(8,128)(2,1)} %param.15) | copy-start | bytes 786436
  38.1 11.3 %copy-start.3 = (f32[1024]{0:T(1024)S(1)}, f32[1024]{0:T(1024)}, u32[]{:S(2)}) copy-start(f32[1024]{0:T(1024)} %param.17) | copy-start | bytes 12292
  38.1 11.1 %all-to-all-start = ((f32[4,128,256]{2,1,0:T(8,128)}), f32[4,128,256]{2,1,0:T(8,128)S(1)}, u32[]{:S(2)}, u32[]{:S(2)}) async-start(f32[4,128,256]{2,1,0:T(8,128)} %bitcast), calls=%async_computation | async-start | bytes 1048576 | tf_op jit(solution)/shard_map/all_to_all | solution.py:40
  96.7 2.4 %copy-start.7 = (bf16[1,512,1024]{2,1,0:T(8,128)(2,1)S(1)}, bf16[1,512,1024]{2,1,0:T(8,128)(2,1)}, u32[]{:S(2)}) copy-start(bf16[1,512,1024]{2,1,0:T(8,128)(2,1)} %param.20) | copy-start | bytes 3145732
  101.7 5.7 %copy-start.5 = (f32[128,8]{0,1:T(8,128)S(1)}, f32[128,8]{0,1:T(8,128)}, u32[]{:S(2)}) copy-start(f32[128,8]{0,1:T(8,128)} %param.27) | copy-start | bytes 12292
  101.7 35.9 %all-to-all-start.2 = ((bf16[128,8,1024]{2,1,0:T(8,128)(2,1)}), bf16[128,8,1024]{2,1,0:T(8,128)(2,1)}, u32[]{:S(2)}, u32[]{:S(2)}) async-start(bf16[128,8,1024]{2,1,0:T(8,128)(2,1)} %convert_bitcast_fusion), calls=%async_computation.2 | async-start | bytes 4194304 | tf_op jit(solution)/shard_map/all_to_all | solution.py:98
  145.5 2.5 %copy-start.4 = (f32[1024]{0:T(1024)S(1)}, f32[1024]{0:T(1024)}, u32[]{:S(2)}) copy-start(f32[1024]{0:T(1024)} %param.18) | copy-start | bytes 12292
Sparse Core Ops, SparseCore 0:
  9.0 26.5 all-gather.1
where the time goes:
time: 156 us
  waiting for transfers between devices  48.6 us (31%)
  blocking collectives  40.3 us (26%)
  local copies, waits for them, and re-layouts  29.5 us (19%)
  between operations  13.6 us (9%)
  matrix products  9.91 us (6%)
  starting transfers between devices  9.14 us (6%)
  other arithmetic  4.53 us (3%)
    all_to_all x1, blocking collectives, on_device(): lax.all_to_all(buffer.reshape(devices_all, cap_size, features), ('grp', '...  40.3 us
    all_to_all x1, waiting for transfers between devices, on_device(): lax.all_to_all(produced.reshape(arrived.shape), ('grp', 'ep'), split_axis...  29.9 us
    all_gather x1, waiting for transfers between devices, on_device(): lax.all_gather(attention, 'grp', axis=0, tiled=True)  10.7 us
    gather x1, local copies, waits for them, and re-layouts, on_device(): expert_out = flat_back[jnp.minimum(index, total_slots - 1)]  7.92 us
    all_to_all x1, waiting for transfers between devices, on_device(): lax.all_to_all(columns, 'grp', split_axis=0, concat_axis=1, tiled=True)  7.26 us
    gather x5, local copies, waits for them, and re-layouts, on_device(): position = jnp.take_along_axis(counts, target, axis=1).astype(jnp.int32)  7.12 us
    scatter x1, local copies, waits for them, and re-layouts, on_device(): buffer = jnp.zeros((total_slots, features), jnp.bfloat16).at[index.reshap...  6.83 us
    gather x3, local copies, waits for them, and re-layouts, on_device(): granted = jnp.take(capacity.reshape(-1), target)  6.7 us
  transfers between devices with their start and end apart: 3, of which 3 were waited for; matrix products, arithmetic and copies ran while one was open for 12% of the time, Pallas kernels for 0%

commit v1 on v0

--- a/solution.py
+++ b/solution.py
@@ -33,7 +33,9 @@
     picks_row = expert_ids.shape[1]
     cap_size = max(2, rows_here * picks_row // devices_all)
     columns = jnp.dot(
-        lax.all_gather(attention, "grp", axis=0, tiled=True),
+        jnp.concatenate(
+            lax.all_to_all(jnp.stack([attention] * lax.axis_size("grp")), "grp", 0, 0), axis=0
+        ),
         out_proj,
         preferred_element_type=jnp.float32,
     )

time: 156 us -> 139 us (0.89)
  between operations: 13.6 us -> 0.27 us
  waiting for transfers between devices: 48.6 us -> 36.3 us
  starting transfers between devices: 9.14 us -> 15.8 us
  local copies, waits for them, and re-layouts: 29.5 us -> 34.2 us
  matrix products: 9.91 us -> 7.47 us
    all_gather x1 -> x0, waiting for transfers between devices: 10.7 us -> none  [on_device(): lax.all_gather(attention, 'grp', axis=0, tiled=True)]
    all_to_all x0 -> x1, starting transfers between devices: none -> 5.86 us  [on_device(): lax.all_to_all(jnp.stack([attention] * lax.axis_size('grp')), 'grp', 0, 0)]
    unnamed x0 -> x1, other arithmetic: none -> 2.92 us
    dot_general x2 -> x1, matrix products: 4.76 us -> 2.29 us  [on_device(): jnp.dot(jnp.concatenate(lax.all_to_all(jnp.stack([attention] * lax.axis_s...]
    another operation x0 -> x1, local copies, waits for them, and re-layouts: none -> 2.21 us  [on_device(): jnp.stack([attention] * lax.axis_size('grp'))]
  transfers between devices with their start and end apart: 3 -> 3, of which waited for: 3 -> 2; matrix products, arithmetic and copies ran while one was open for 12% -> 12% of each run, Pallas kernels for 0% -> 0%
where the time goes in v1:
time: 139 us
  blocking collectives  40.4 us (29%)
  waiting for transfers between devices  36.3 us (26%)
  local copies, waits for them, and re-layouts  34.2 us (25%)
  starting transfers between devices  15.8 us (11%)
  matrix products  7.47 us (5%)
  other arithmetic  4.16 us (3%)
    all_to_all x1, blocking collectives, on_device(): lax.all_to_all(buffer.reshape(devices_all, cap_size, features), ('grp', '...  40.4 us
    all_to_all x1, waiting for transfers between devices, on_device(): lax.all_to_all(produced.reshape(arrived.shape), ('grp', 'ep'), split_axis...  30 us
    gather x1, local copies, waits for them, and re-layouts, on_device(): expert_out = flat_back[jnp.minimum(index, total_slots - 1)]  7.94 us
    gather x5, local copies, waits for them, and re-layouts, on_device(): position = jnp.take_along_axis(counts, target, axis=1).astype(jnp.int32)  7.12 us
    scatter x1, local copies, waits for them, and re-layouts, on_device(): buffer = jnp.zeros((total_slots, features), jnp.bfloat16).at[index.reshap...  6.83 us
    gather x3, local copies, waits for them, and re-layouts, on_device(): granted = jnp.take(capacity.reshape(-1), target)  6.69 us
    all_to_all x1, waiting for transfers between devices, on_device(): lax.all_to_all(columns, 'grp', split_axis=0, concat_axis=1, tiled=True)  6.34 us
    all_to_all x1, starting transfers between devices, on_device(): lax.all_to_all(jnp.stack([attention] * lax.axis_size('grp')), 'grp', 0, 0)  5.86 us
  transfers between devices with their start and end apart: 3, of which 2 were waited for; matrix products, arithmetic and copies ran while one was open for 12% of the time, Pallas kernels for 0%

profile of v1, /device:TPU:1, one launch (start us, length us, event | category | flops | bytes accessed | tf_op | source)
XLA Modules:
  0.0 138.6 jit_solution(17095878688669678342)
XLA Ops:
  0.0 0.0 copy-start
  0.0 0.0 copy-start.8
  0.0 0.0 copy-start.3
  0.0 0.0 copy-start.5
  0.0 0.0 copy-start.9
  0.0 0.0 copy-start.10
  0.0 2.2 %stack.2 = bf16[4,128,1024]{2,1,0:T(8,128)(2,1)} broadcast(bf16[128,1024]{1,0:T(8,128)(2,1)} %param.14), dimensions={1,2} | broadcast | bytes 1310720 | tf_op jit(solution)/shard_map/stack | solution.py:37
  2.2 5.9 %all-to-all-start = ((bf16[4,128,1024]{2,1,0:T(8,128)(2,1)}), bf16[4,128,1024]{2,1,0:T(8,128)(2,1)S(1)}, u32[]{:S(2)}, u32[]{:S(2)}) async-start(bf16[4,128,1024]{2,1,0:T(8,128)(2,1)} %stack.2), calls=%async_computation | async-start | bytes 2097152 | tf_op jit(solution)/shard_map/all_to_all | solution.py:37
  8.1 0.0 copy-done.8
  8.1 0.1 select_reduce_fusion.1
  8.2 0.0 copy-done.3
  8.2 0.1 select_reduce_fusion
  8.3 0.0 copy-done.5
  8.3 0.1 copy.27
  8.4 0.1 copy.28
  8.6 0.1 reshape.115
  8.6 0.0 copy-done.9
  8.7 0.0 copy-done.10
  8.7 0.2 fusion.18
  8.9 0.2 fusion.21
  9.1 0.0 copy-start.6
  9.1 6.8 %gather_fusion.2 = f32[1024]{0:T(1024)S(1)} fusion(f32[128,128]{1,0:T(8,128)S(1)} %fusion.21, s32[1024]{0:T(1024)S(1)} %reshape.115), kind=kCustom, calls=%fused_computation.2 | custom fusion | bytes 16384 | tf_op jit(solution)/shard_map/jit(take_along_axis)/gather | solution.py:69
  15.9 0.1 reshape.118
  16.1 0.1 copy.30
  16.2 0.1 reshape.101
  16.3 0.0 copy-done.6
  16.3 0.1 reshape.92
  16.4 6.6 %gather_fusion = s32[1024]{0:T(1024)S(1)} fusion(s32[128]{0:T(128)S(1)} %reshape.92, s32[1024]{0:T(1024)S(1)} %broadcast_clamp_fusion.1), kind=kCustom, calls=%fused_computation | custom fusion | bytes 12288 | tf_op jit(solution)/shard_map/jit(_take)/gather | solution.py:70
  23.0 0.1 reshape.100
  23.1 0.0 all-to-all-done
  23.1 2.3 %fusion.15 = f32[4,128,256]{2,1,0:T(8,128)} fusion(bf16[4,128,1024]{2,1,0:T(8,128)(2,1)S(1)} %all-to-all-done, bf16[1024,256]{1,0:T(8,128)(2,1)} %param.16), kind=kOutput, calls=%fused_computation.25 | convolution fusion | flops 268435456 | bytes 2097152 | tf_op jit(solution)/shard_map/dot_general | solution.py:35
  25.4 0.0 copy-start.1
  25.4 4.4 %all-to-all-start.1 = ((f32[4,128,256]{2,1,0:T(8,128)}), f32[4,128,256]{2,1,0:T(8,128)S(1)}, u32[]{:S(2)}, u32[]{:S(2)}) async-start(f32[4,128,256]{2,1,0:T(8,128)} %fusion.15), calls=%async_computation.1 | async-start | bytes 1048576 | tf_op jit(solution)/shard_map/all_to_all | solution.py:42
  29.8 0.1 copy.32
  29.9 0.1 reshape.93
  30.0 1.1 copy.25
  31.1 6.3 %all-to-all-done.1 = f32[4,128,256]{2,1,0:T(8,128)S(1)} async-done(((f32[4,128,256]{2,1,0:T(8,128)}), f32[4,128,256]{2,1,0:T(8,128)S(1)}, u32[]{:S(2)}, u32[]{:S(2)}) %all-to-all-start.1) | async-done | bytes 524320 | tf_op jit(solution)/shard_map/all_to_all | solution.py:42
  37.5 0.2 copy.26
  37.7 0.2 fusion.11
  37.8 0.0 copy-done.1
  37.8 0.2 fusion.13
  38.1 0.1 copy.33
  38.2 6.8 %scatter_custom_fusion = bf16[1024,1024]{1,0:T(8,128)(2,1)} fusion(s32[1024]{0:T(1024)S(1)} %bitcast.36, bf16[128,1024]{1,0:T(8,128)(2,1)S(1)} %copy.33, bf16[]{:T(256)} %constant.29.clone.1), kind=kCustom, calls=%fused_computation.10 | custom fusion | bytes 2359298 | tf_op jit(solution)/shard_map/scatter | solution.py:80
  45.0 40.4 %all_to_all.31 = bf16[128,8,1024]{2,1,0:T(8,128)(2,1)S(1)} all-to-all(bf16[128,8,1024]{2,1,0:T(8,128)(2,1)} %bitcast.34), channel_id=1, replica_groups=mesh['grp'=4,'ep'=32] {'grp','ep'}, dimensions={0} | all-to-all | bytes 4194304 | tf_op jit(solution)/shard_map/all_to_all | solution.py:85
  85.4 0.0 copy-done
  85.4 0.0 copy-start.7
  85.4 2.4 %fusion.1 = f32[1024,1024]{1,0:T(8,128)S(1)} fusion(bf16[1,1024,1024]{2,1,0:T(8,128)(2,1)S(1)} %copy-done, bf16[128,8,1024]{2,1,0:T(8,128)(2,1)S(1)} %all_to_all.31), kind=kOutput, calls=%fused_computation.7 | convolution fusion | flops 2147483648 | bytes 8388608 | tf_op jit(solution)/shard_map/dot_general | solution.py:93
  87.8 0.0 copy-done.7
  87.8 2.6 %convert_bitcast_fusion = bf16[128,8,1024]{2,1,0:T(8,128)(2,1)} fusion(f32[1024,1024]{1,0:T(8,128)S(1)} %fusion.1, bf16[1,512,1024]{2,1,0:T(8,128)(2,1)S(1)} %copy-done.7), kind=kOutput, calls=%fused_computation.12 | convolution fusion | flops 1077936128 | bytes 7340032 | tf_op jit(solution)/shard_map/dot_general | solution.py:97
  90.4 0.0 copy-start.4
  90.4 5.5 %all-to-all-start.3 = ((bf16[128,8,1024]{2,1,0:T(8,128)(2,1)}), bf16[128,8,1024]{2,1,0:T(8,128)(2,1)}, u32[]{:S(2)}, u32[]{:S(2)}) async-start(bf16[128,8,1024]{2,1,0:T(8,128)(2,1)} %convert_bitcast_fusion), calls=%async_computation.3 | async-start | bytes 4194304 | tf_op jit(solution)/shard_map/all_to_all | solution.py:100
  96.0 0.1 copy.34
  96.1 0.1 reshape.109
  96.2 0.0 copy-done.4
  96.2 0.1 copy.40
  96.3 30.0 %all-to-all-done.3 = bf16[128,8,1024]{2,1,0:T(8,128)(2,1)} async-done(((bf16[128,8,1024]{2,1,0:T(8,128)(2,1)}), bf16[128,8,1024]{2,1,0:T(8,128)(2,1)}, u32[]{:S(2)}, u32[]{:S(2)}) %all-to-all-start.3) | async-done | bytes 2097184 | tf_op jit(solution)/shard_map/all_to_all | solution.py:100
  126.3 7.9 %gather_fusion.1 = bf16[1024,1024]{1,0:T(8,128)(2,1)} fusion(bf16[1024,1024]{1,0:T(8,128)(2,1)} %bitcast.11, s32[1024]{0:T(1024)S(1)} %broadcast_clamp_fusion), kind=kCustom, calls=%fused_computation.1 | custom fusion | bytes 4198400 | tf_op jit(solution)/shard_map/gather | solution.py:104
  134.2 0.0 copy-start.2
  134.2 2.9 %multiply_reduce_fusion = f32[128,1024]{1,0:T(8,128)S(1)} fusion(f32[128,8]{1,0:T(8,128)S(1)} %copy.40, bf16[1024,1024]{1,0:T(8,128)(2,1)} %gather_fusion.1), kind=kLoop, calls=%fused_computation.4 | loop fusion | flops 3014656 | bytes 2625536
  137.1 0.2 copy.39
  137.3 0.2 multiply_reduce_fusion.1
  137.5 0.0 copy-done.2
  137.5 0.2 multiply_convert_fusion
  137.7 0.9 copy.35
  (12 shorter events, 0.2 us)
Async XLA Ops:
  0.0 85.4 %copy-start = (bf16[1,1024,1024]{2,1,0:T(8,128)(2,1)S(1)}, bf16[1,1024,1024]{2,1,0:T(8,128)(2,1)}, u32[]{:S(2)}) copy-start(bf16[1,1024,1024]{2,1,0:T(8,128)(2,1)} %param.19) | copy-start | bytes 6291460
  0.0 8.1 %copy-start.8 = (s32[32]{0:T(128)S(1)}, s32[32]{0:T(128)}, u32[]{:S(2)}) copy-start(s32[32]{0:T(128)} %param.23) | copy-start | bytes 388
  0.0 8.2 %copy-start.3 = (s32[128,8]{0,1:T(8,128)S(1)}, s32[128,8]{0,1:T(8,128)}, u32[]{:S(2)}) copy-start(s32[128,8]{0,1:T(8,128)} %param.21) | copy-start | bytes 12292
  0.0 8.3 %copy-start.5 = (s32[128,8]{0,1:T(8,128)S(1)}, s32[128,8]{0,1:T(8,128)}, u32[]{:S(2)}) copy-start(s32[128,8]{0,1:T(8,128)} %param.22) | copy-start | bytes 12292
  0.0 8.6 %copy-start.9 = (s32[128]{0:T(128)S(1)}, s32[128]{0:T(128)}, u32[]{:S(2)}) copy-start(s32[128]{0:T(128)} %param.24) | copy-start | bytes 1540
  0.0 8.6 %copy-start.10 = (s32[128]{0:T(128)S(1)}, s32[128]{0:T(128)}, u32[]{:S(2)}) copy-start(s32[128]{0:T(128)} %param.25) | copy-start | bytes 1540
  2.2 20.9 %all-to-all-start = ((bf16[4,128,1024]{2,1,0:T(8,128)(2,1)}), bf16[4,128,1024]{2,1,0:T(8,128)(2,1)S(1)}, u32[]{:S(2)}, u32[]{:S(2)}) async-start(bf16[4,128,1024]{2,1,0:T(8,128)(2,1)} %stack.2), calls=%async_computation | async-start | bytes 2097152 | tf_op jit(solution)/shard_map/all_to_all | solution.py:37
  9.1 7.2 %copy-start.6 = (s32[4,32]{1,0:T(4,128)S(1)}, s32[4,32]{1,0:T(4,128)}, u32[]{:S(2)}) copy-start(s32[4,32]{1,0:T(4,128)} %param.26) | copy-start | bytes 1540
  25.4 12.4 %copy-start.1 = (f32[1024]{0:T(1024)S(1)}, f32[1024]{0:T(1024)}, u32[]{:S(2)}) copy-start(f32[1024]{0:T(1024)} %param.17) | copy-start | bytes 12292
  25.4 12.1 %all-to-all-start.1 = ((f32[4,128,256]{2,1,0:T(8,128)}), f32[4,128,256]{2,1,0:T(8,128)S(1)}, u32[]{:S(2)}, u32[]{:S(2)}) async-start(f32[4,128,256]{2,1,0:T(8,128)} %fusion.15), calls=%async_computation.1 | async-start | bytes 1048576 | tf_op jit(solution)/shard_map/all_to_all | solution.py:42
  85.4 2.4 %copy-start.7 = (bf16[1,512,1024]{2,1,0:T(8,128)(2,1)S(1)}, bf16[1,512,1024]{2,1,0:T(8,128)(2,1)}, u32[]{:S(2)}) copy-start(bf16[1,512,1024]{2,1,0:T(8,128)(2,1)} %param.20) | copy-start | bytes 3145732
  90.4 5.8 %copy-start.4 = (f32[128,8]{0,1:T(8,128)S(1)}, f32[128,8]{0,1:T(8,128)}, u32[]{:S(2)}) copy-start(f32[128,8]{0,1:T(8,128)} %param.27) | copy-start | bytes 12292
  90.4 35.8 %all-to-all-start.3 = ((bf16[128,8,1024]{2,1,0:T(8,128)(2,1)}), bf16[128,8,1024]{2,1,0:T(8,128)(2,1)}, u32[]{:S(2)}, u32[]{:S(2)}) async-start(bf16[128,8,1024]{2,1,0:T(8,128)(2,1)} %convert_bitcast_fusion), calls=%async_computation.3 | async-start | bytes 4194304 | tf_op jit(solution)/shard_map/all_to_all | solution.py:100
  134.2 3.3 %copy-start.2 = (f32[1024]{0:T(1024)S(1)}, f32[1024]{0:T(1024)}, u32[]{:S(2)}) copy-start(f32[1024]{0:T(1024)} %param.18) | copy-start | bytes 12292
